TPU v7x, 512 devices: a whole 4x8x8 slice. The times are simulated.
512 devices in a mesh: dp: 64 (over z, y), mp: 8 (over x, core).
Axes of the slice: x: 4, y: 8, z: 8, core: 2. Of those that a mesh axis runs over, the one named last changes fastest.
Arguments:
- spikes: bfloat16 [3584, 16, 384], P('dp'), may hold values from -6 to 6
- session_ids: int32 [3584, 1], P('dp'), may hold values from 0 to 63; in each aligned block of 56 rows (0 to 55, 56 to 111, ...) at most 2 rows name the same one
- readin: bfloat16 [64, 384, 4096], P('dp', None, 'mp')
- gain: float32 [4096], P('mp'), may hold values from 0.5 to 1.5
- proj: bfloat16 [4096, 2048], P('mp', 'dp'), may hold values from -0.09375 to 0.09375
- query_bias: float32 [2048], P('mp'), may hold values from -1.5 to 1.5
- cotangent: bfloat16 [3584, 16, 2048], P('dp', None, 'mp'), may hold values from -0.0234375 to 0.0234375
Outputs:
- readin_grad: float32 [64, 384, 4096], P('dp', None, 'mp')
- gain_grad: float32 [4096], P('mp')
- proj_grad: float32 [4096, 2048], P('mp', 'dp')
Inputs may be any that keep to these rules, and one draw needn't show every extreme that they name: `session_ids`: among the 56 windows of one device no session appears more than 2 times, and some session appears exactly 2 times.
All inputs are finite; a program needn't handle non-finite values.
Results may differ from a plain program's by a relative error of at most 0.011.
Values may be sent and summed in bfloat16 or wider, within the bound.
A program may use at most 64 MiB of HBM per device.

v0:
```python
import jax
import jax.numpy as jnp
from jax import lax
from jax.sharding import PartitionSpec as P

D = 4096
HD = 128
MOST = 2
eps_norm = 1e-05


def on_device(spikes, session_ids, readin, gain, proj, query_bias, cotangent):
    windows, bin_count, channels = spikes.shape
    owner_count = lax.axis_size("dp")
    slot_count = owner_count * MOST
    slice_width = readin.shape[2]
    row_count = windows * bin_count
    share = cotangent.shape[2]
    owners = session_ids[:, 0]
    positions = jnp.arange(windows)
    earlier = (owners[:, None] == owners[None, :]) & (positions[None, :] < positions[:, None])
    ranked = jnp.sum(earlier.astype(jnp.int32), axis=1)
    target = owners * MOST + ranked
    placing = (jnp.arange(slot_count)[:, None] == target[None, :]).astype(jnp.bfloat16)
    outgoing = jnp.dot(
        placing, spikes.reshape(windows, bin_count * channels), preferred_element_type=jnp.float32
    )
    outgoing = outgoing.astype(jnp.bfloat16).reshape(owner_count, MOST, bin_count, channels)
    table = readin[0]
    arrived = lax.all_to_all(outgoing, "dp", split_axis=0, concat_axis=0, tiled=True)
    items = arrived.shape[1]
    mapped = jnp.dot(arrived.reshape(-1, channels), table, preferred_element_type=jnp.float32)
    mapped = mapped.astype(jnp.bfloat16).reshape(owner_count, items, bin_count, slice_width)
    returned = lax.all_to_all(mapped, "dp", split_axis=0, concat_axis=0, tiled=True)
    returned, arrived = (returned, arrived)
    gathered_rows = lax.dot_general(
        placing,
        returned.reshape(slot_count, bin_count * slice_width),
        (((0,), (0,)), ((), ())),
        preferred_element_type=jnp.float32,
    )
    features = gathered_rows.reshape(row_count, slice_width)
    squares = lax.psum(jnp.sum(features * features, axis=-1), "mp")
    inverse = lax.rsqrt(squares / D + eps_norm)[:, None]
    normed = (features * inverse * gain).astype(jnp.bfloat16)
    whole_proj = lax.all_gather(proj, "dp", axis=1, tiled=True)
    partial_queries = jnp.dot(normed, whole_proj, preferred_element_type=jnp.float32)
    summed = lax.psum(partial_queries.astype(jnp.bfloat16), "mp").astype(jnp.float32)
    own_queries = lax.dynamic_slice_in_dim(summed, lax.axis_index("mp") * share, share, 1)
    own_queries = own_queries + query_bias
    queries = own_queries.reshape(row_count, share // HD, HD)
    scale = lax.rsqrt(jnp.mean(queries * queries, axis=-1, keepdims=True) + eps_norm)
    unit = queries * scale
    upstream = cotangent.reshape(row_count, share // HD, HD).astype(jnp.float32)
    own_grad = scale * (upstream - unit * jnp.mean(upstream * unit, axis=-1, keepdims=True))
    own_grad = own_grad.reshape(row_count, share).astype(jnp.bfloat16)
    query_grad = lax.all_gather(own_grad, "mp", axis=1, tiled=True)
    proj_grad = lax.psum_scatter(
        lax.dot_general(
            query_grad, normed, (((0,), (0,)), ((), ())), preferred_element_type=jnp.float32
        ),
        "dp",
        scatter_dimension=0,
        tiled=True,
    ).T
    normed_grad = lax.dot_general(
        query_grad, whole_proj, (((1,), (1,)), ((), ())), preferred_element_type=jnp.float32
    )
    scaled_grad = gain * normed_grad
    cross_sums = lax.psum(jnp.sum(scaled_grad * features, axis=-1), "mp")
    feature_grad = inverse * scaled_grad - features * inverse**3 * (cross_sums / D)[:, None]
    feature_grad = feature_grad.astype(jnp.bfloat16).reshape(windows, bin_count * slice_width)
    local_gain = jnp.sum(normed_grad * features * inverse, axis=0)
    gain_grad = lax.psum(local_gain, "dp")
    slotted = jnp.dot(placing, feature_grad, preferred_element_type=jnp.float32)
    slotted = slotted.astype(jnp.bfloat16).reshape(owner_count, MOST, bin_count, slice_width)
    incoming = lax.all_to_all(slotted, "dp", split_axis=0, concat_axis=0, tiled=True)
    readin_grad = lax.dot_general(
        arrived.reshape(-1, channels),
        incoming.reshape(-1, slice_width),
        (((0,), (0,)), ((), ())),
        preferred_element_type=jnp.float32,
    )
    return (readin_grad[None], gain_grad, proj_grad)


def solution(mesh):
    return jax.shard_map(
        on_device,
        mesh=mesh,
        in_specs=(
            P("dp", None, None),
            P("dp", None),
            P("dp", None, "mp"),
            P("mp"),
            P("mp", "dp"),
            P("mp"),
            P("dp", None, "mp"),
        ),
        out_specs=(P("dp", None, "mp"), P("mp"), P("mp", "dp")),
        check_vma=False,
    )
```

profile of v0, /device:TPU:2, one launch (start us, length us, event | category | flops | bytes accessed | tf_op | source)
XLA Modules:
  0.0 636.0 jit_solution(13360322924819784834)
XLA Ops:
  7.2 0.9 convert_reduce_fusion
  8.8 1.2 copy.18
  10.9 57.7 %all_to_all.15 = bf16[64,2,16,384]{3,2,1,0:T(8,128)(2,1)S(1)} all-to-all(bf16[64,2,16,384]{3,2,1,0:T(8,128)(2,1)S(1)} %bitcast.56), channel_id=1, replica_groups=mesh['dp'=64,'mp'=8] {'dp'}, dimensions={0} | all-to-all | bytes 3145728 | tf_op jit(solution)/shard_map/all_to_all | solution.py:30
  68.5 2.6 convolution_convert_fusion.3
  71.2 7.6 %all-to-all-start.1 = ((bf16[64,2,16,512]{3,2,1,0:T(8,128)(2,1)}), bf16[64,2,16,512]{3,2,1,0:T(8,128)(2,1)S(1)}, u32[]{:S(2)}, u32[]{:S(2)}) async-start(bf16[64,2,16,512]{3,2,1,0:T(8,128)(2,1)} %bitcast.60), calls=%async_computation.1 | async-start | bytes 4194304 | tf_op jit(solution)/shard_map/all_to_all | solution.py:34
  79.5 51.1 %all-to-all-done.1 = bf16[64,2,16,512]{3,2,1,0:T(8,128)(2,1)S(1)} async-done(((bf16[64,2,16,512]{3,2,1,0:T(8,128)(2,1)}), bf16[64,2,16,512]{3,2,1,0:T(8,128)(2,1)S(1)}, u32[]{:S(2)}, u32[]{:S(2)}) %all-to-all-start.1) | async-done | bytes 2097184 | tf_op jit(solution)/shard_map/all_to_all | solution.py:34
  130.7 1.4 copy.20
  132.0 1.7 fusion.4
  133.8 1.6 reshape.78
  135.6 10.4 %psum.28 = f32[896]{0:T(1024)S(1)} all-reduce(f32[896]{0:T(1024)S(1)} %multiply_reduce_fusion.2), channel_id=1, replica_groups=mesh['dp'=64,'mp'=8] {'mp'}, use_global_device_ids=true, to_apply=%region_2.0 | all-reduce | flops 896 | bytes 7168 | tf_op jit(solution)/shard_map/psum | solution.py:43
  146.0 39.0 %all-gather.3.cloned.1.call-done = bf16[512,2048]{0,1:T(8,128)(2,1)} async-done(((bf16[512,32]{0,1:T(8,128)(2,1)}), bf16[512,2048]{0,1:T(8,128)(2,1)}) %all-gather.3.cloned.1.call-update) | async-done | bytes 2097168 | tf_op jit(solution)/shard_map/all_gather | solution.py:46
  185.0 5.6 convolution_convert_fusion.2
  190.8 0.8 copy-done.2
  191.6 1.4 reshape.83
  193.0 73.4 %all-reduce.2.cloned.1.call-done = bf16[896,2048]{1,0:T(8,128)(2,1)} async-done(((bf16[896,2048]{1,0:T(8,128)(2,1)}), bf16[896,2048]{1,0:T(8,128)(2,1)}) %all-reduce.2.cloned.1.call-update) | async-done | bytes 3670032 | tf_op jit(solution)/shard_map/psum | solution.py:48
  266.4 2.0 convert_add_fusion
  268.4 1.6 reshape.79
  270.1 1.0 multiply_reduce_fusion.4
  271.3 12.7 %multiply_reduce_fusion.3 = f32[896,2]{1,0:T(8,128)S(1)} fusion(f32[896,2,128]{2,1,0:T(2,128)S(1)} %copy-done.1, f32[896,2,128]{2,1,0:T(2,128)S(1)} %reshape.79, f32[896,2]{1,0:T(8,128)S(1)} %add_rsqrt_fusion), kind=kLoop, calls=%fused_computation.15 | loop fusion | flops 686336 | bytes 1849344 | tf_op jit(solution)/shard_map/reduce_sum | solution.py:55
  284.0 1.1 mul.123
  285.1 1.1 mul.118
  286.2 2.1 fusion.2
  288.3 41.5 %all-gather.5.cloned.1.call-done = bf16[896,2048]{1,0:T(8,128)(2,1)} async-done(((bf16[896,256]{1,0:T(8,128)(2,1)}), bf16[896,2048]{1,0:T(8,128)(2,1)}) %all-gather.5.cloned.1.call-update) | async-done | bytes 3670032 | tf_op jit(solution)/shard_map/all_gather | solution.py:57
  329.8 6.4 %fusion.9 = f32[2048,512]{1,0:T(8,128)} fusion(bf16[896,2048]{1,0:T(8,128)(2,1)} %all-gather.5.cloned.1.call-done, f32[896,512]{1,0:T(8,128)S(1)} %reshape.78, f32[512]{0:T(512)S(1)} %copy-done.6, f32[896]{0:T(1024)S(1)} %get-tuple-element.6), kind=kOutput, calls=%fused_computation.33 | convolution fusion | flops 1880424448 | bytes 9704960 | tf_op jit(solution)/shard_map/dot_general | solution.py:59
  336.3 6.1 multiply_reduce_fusion
  342.4 12.0 %psum.30 = f32[896]{0:T(1024)S(1)} all-reduce(f32[896]{0:T(1024)S(1)} %get-tuple-element.4), channel_id=1, replica_groups=mesh['dp'=64,'mp'=8] {'mp'}, use_global_device_ids=true, to_apply=%region_7.0 | all-reduce | flops 896 | bytes 7168 | tf_op jit(solution)/shard_map/psum | solution.py:70
  354.4 1.9 subtract_convert_fusion
  357.4 2.2 copy.23
  359.6 13.3 %all-to-all-start.2 = ((bf16[64,2,16,512]{3,2,1,0:T(8,128)(2,1)}), bf16[64,2,16,512]{3,2,1,0:T(8,128)(2,1)S(1)}, u32[]{:S(2)}, u32[]{:S(2)}) async-start(bf16[64,2,16,512]{3,2,1,0:T(8,128)(2,1)} %bitcast.25), calls=%async_computation.2 | async-start | bytes 4194304 | tf_op jit(solution)/shard_map/all_to_all | solution.py:77
  372.9 181.6 %psum.31 = f32[512]{0:T(512)} all-reduce(f32[512]{0:T(512)S(1)} %get-tuple-element.3), channel_id=1, replica_groups=mesh['dp'=64,'mp'=8] {'dp'}, use_global_device_ids=true, to_apply=%region_9.0 | all-reduce | flops 512 | bytes 4096 | tf_op jit(solution)/shard_map/psum | solution.py:74
  554.5 3.3 convolution_bitcast_fusion
  557.8 71.7 %reduce-scatter.2.cloned.1.call-done = f32[32,512]{1,0:T(8,128)} async-done(((f32[2048,512]{1,0:T(8,128)}), f32[32,512]{1,0:T(8,128)}) %reduce-scatter.2.cloned.1.call-update) | async-done | bytes 65552 | tf_op jit(solution)/shard_map/reduce_scatter | solution.py:58
  (32 shorter events, 4.1 us)
Async XLA Ops:
  7.2 61.4 %copy-start = (bf16[1,384,512]{2,1,0:T(8,128)(2,1)S(1)}, bf16[1,384,512]{2,1,0:T(8,128)(2,1)}, u32[]{:S(2)}) copy-start(bf16[1,384,512]{2,1,0:T(8,128)(2,1)} %param.9) | copy-start | bytes 1179652
  68.5 2.6 copy-start.4
  71.2 59.5 %all-to-all-start.1 = ((bf16[64,2,16,512]{3,2,1,0:T(8,128)(2,1)}), bf16[64,2,16,512]{3,2,1,0:T(8,128)(2,1)S(1)}, u32[]{:S(2)}, u32[]{:S(2)}) async-start(bf16[64,2,16,512]{3,2,1,0:T(8,128)(2,1)} %bitcast.60), calls=%async_computation.1 | async-start | bytes 4194304 | tf_op jit(solution)/shard_map/all_to_all | solution.py:34
  78.8 106.3 %all-gather.3.cloned.1.call-start = ((), (), s32[]{:S(2)}) async-start(), calls=%async_computation.4 | async-start | bytes 2129920 | tf_op jit(solution)/shard_map/all_gather | solution.py:46
  79.5 186.9 %all-reduce.2.cloned.1.call-start = ((), (), s32[]{:S(2)}) async-start(), calls=%async_computation.5 | async-start | bytes 7340032 | tf_op jit(solution)/shard_map/psum | solution.py:48
  135.4 49.6 %copy-start.6 = (f32[512]{0:T(512)S(1)}, f32[512]{0:T(512)}, u32[]{:S(2)}) copy-start(f32[512]{0:T(512)} %param.10) | copy-start | bytes 6148
  190.6 1.0 copy-start.2
  190.6 75.8 %copy-start.5 = (f32[256]{0:T(256)S(1)}, f32[256]{0:T(256)}, u32[]{:S(2)}) copy-start(f32[256]{0:T(256)} %param.12) | copy-start | bytes 3076
  190.6 139.2 %all-gather.5.cloned.1.call-start = ((), (), s32[]{:S(2)}) async-start(), calls=%async_computation.6 | async-start | bytes 4128768 | tf_op jit(solution)/shard_map/all_gather | solution.py:57
  270.1 1.2 copy-start.1
  283.9 2.3 copy-start.3
  288.3 341.2 %reduce-scatter.2.cloned.1.call-start = ((), (), s32[]{:S(2)}) async-start(), calls=%async_computation.7 | async-start | bytes 4259840 | tf_op jit(solution)/shard_map/reduce_scatter | solution.py:58
  359.6 194.9 %all-to-all-start.2 = ((bf16[64,2,16,512]{3,2,1,0:T(8,128)(2,1)}), bf16[64,2,16,512]{3,2,1,0:T(8,128)(2,1)S(1)}, u32[]{:S(2)}, u32[]{:S(2)}) async-start(bf16[64,2,16,512]{3,2,1,0:T(8,128)(2,1)} %bitcast.25), calls=%async_computation.2 | async-start | bytes 4194304 | tf_op jit(solution)/shard_map/all_to_all | solution.py:77
Sparse Core Ops, SparseCore 0:
  82.7 102.3 all-gather.2
  190.7 75.6 all-reduce.1
  288.4 41.3 all-gather.4
  336.4 293.0 reduce-scatter.1
where the time goes:
time: 637 us; the launch traced here: 636 us
  waiting for transfers between devices  277 us (43%)
  blocking collectives  262 us (41%)
  matrix products  27 us (4%)
  other arithmetic  21.6 us (3%)
  starting transfers between devices  21.2 us (3%)
  between operations  13.9 us (2%)
  local copies, waits for them, and re-layouts  13.2 us (2%)
    psum x1, blocking collectives, on_device(): gain_grad = lax.psum(local_gain, 'dp')  182 us
    psum x1, waiting for transfers between devices, on_device(): lax.psum(partial_queries.astype(jnp.bfloat16), 'mp').astype(jnp.float32)  73.4 us
    reduce_scatter x1, waiting for transfers between devices, on_device(): lax.psum_scatter(lax.dot_general(query_grad, normed, (((0,), (0,)), ((),...  71.7 us
    all_to_all x1, blocking collectives, on_device(): lax.all_to_all(outgoing, 'dp', split_axis=0, concat_axis=0, tiled=True)  57.7 us
    all_to_all x1, waiting for transfers between devices, on_device(): lax.all_to_all(mapped, 'dp', split_axis=0, concat_axis=0, tiled=True)  51.1 us
    all_gather x1, waiting for transfers between devices, on_device(): query_grad = lax.all_gather(own_grad, 'mp', axis=1, tiled=True)  41.5 us
    all_gather x1, waiting for transfers between devices, on_device(): whole_proj = lax.all_gather(proj, 'dp', axis=1, tiled=True)  39 us
    all_to_all x1, starting transfers between devices, on_device(): lax.all_to_all(slotted, 'dp', split_axis=0, concat_axis=0, tiled=True)  13.3 us
  transfers between devices with their start and end apart: 6, of which 5 were waited for; matrix products, arithmetic and copies ran while one was open for 3% of the time, Pallas kernels for 0%

commit v1 on v0

--- a/solution.py
+++ b/solution.py
@@ -45,7 +45,9 @@
     normed = (features * inverse * gain).astype(jnp.bfloat16)
     whole_proj = lax.all_gather(proj, "dp", axis=1, tiled=True)
     partial_queries = jnp.dot(normed, whole_proj, preferred_element_type=jnp.float32)
-    summed = lax.psum(partial_queries.astype(jnp.bfloat16), "mp").astype(jnp.float32)
+    summed = jnp.sum(lax.all_gather(partial_queries.astype(jnp.bfloat16), "mp"), axis=0).astype(
+        jnp.float32
+    )
     own_queries = lax.dynamic_slice_in_dim(summed, lax.axis_index("mp") * share, share, 1)
     own_queries = own_queries + query_bias
     queries = own_queries.reshape(row_count, share // HD, HD)

time: 637 us -> 711 us (1.12)
  waiting for transfers between devices: 277 us -> 338 us
  other arithmetic: 21.6 us -> 34.3 us
    all_gather x0 -> x1, waiting for transfers between devices: none -> 138 us  [on_device(): lax.all_gather(partial_queries.astype(jnp.bfloat16), 'mp')]
    psum x1 -> x0, waiting for transfers between devices: 73.4 us -> none  [on_device(): lax.psum(partial_queries.astype(jnp.bfloat16), 'mp').astype(jnp.float32)]
    reduce_sum x0 -> x1, other arithmetic: none -> 12.7 us  [on_device(): jnp.sum(lax.all_gather(partial_queries.astype(jnp.bfloat16), 'mp'), axis=0)]
where the time goes in v1:
time: 711 us; the launch traced here: 710 us
  waiting for transfers between devices  338 us (48%)
  blocking collectives  262 us (37%)
  other arithmetic  34.3 us (5%)
  matrix products  27.1 us (4%)
  starting transfers between devices  21.2 us (3%)
  between operations  13.9 us (2%)
  local copies, waits for them, and re-layouts  13.2 us (2%)
    psum x1, blocking collectives, on_device(): gain_grad = lax.psum(local_gain, 'dp')  182 us
    all_gather x1, waiting for transfers between devices, on_device(): lax.all_gather(partial_queries.astype(jnp.bfloat16), 'mp')  138 us
    reduce_scatter x1, waiting for transfers between devices, on_device(): lax.psum_scatter(lax.dot_general(query_grad, normed, (((0,), (0,)), ((),...  69.7 us
    all_to_all x1, blocking collectives, on_device(): lax.all_to_all(outgoing, 'dp', split_axis=0, concat_axis=0, tiled=True)  57.7 us
    all_to_all x1, waiting for transfers between devices, on_device(): lax.all_to_all(mapped, 'dp', split_axis=0, concat_axis=0, tiled=True)  51 us
    all_gather x1, waiting for transfers between devices, on_device(): query_grad = lax.all_gather(own_grad, 'mp', axis=1, tiled=True)  39.9 us
    all_gather x1, waiting for transfers between devices, on_device(): whole_proj = lax.all_gather(proj, 'dp', axis=1, tiled=True)  39 us
  transfers between devices with their start and end apart: 6, of which 5 were waited for; matrix products, arithmetic and copies ran while one was open for 3% of the time, Pallas kernels for 0%

profile of v1, /device:TPU:2, one launch (start us, length us, event | category | flops | bytes accessed | tf_op | source)
XLA Modules:
  0.0 710.0 jit_solution(6636761314439321243)
XLA Ops:
  7.2 0.9 convert_reduce_fusion
  8.8 1.2 copy.18
  10.9 57.7 %all_to_all.15 = bf16[64,2,16,384]{3,2,1,0:T(8,128)(2,1)S(1)} all-to-all(bf16[64,2,16,384]{3,2,1,0:T(8,128)(2,1)S(1)} %bitcast.58), channel_id=1, replica_groups=mesh['dp'=64,'mp'=8] {'dp'}, dimensions={0} | all-to-all | bytes 3145728 | tf_op jit(solution)/shard_map/all_to_all | solution.py:30
  68.5 2.6 convolution_convert_fusion.3
  71.2 7.6 %all-to-all-start.1 = ((bf16[64,2,16,512]{3,2,1,0:T(8,128)(2,1)}), bf16[64,2,16,512]{3,2,1,0:T(8,128)(2,1)S(1)}, u32[]{:S(2)}, u32[]{:S(2)}) async-start(bf16[64,2,16,512]{3,2,1,0:T(8,128)(2,1)} %bitcast.62), calls=%async_computation.1 | async-start | bytes 4194304 | tf_op jit(solution)/shard_map/all_to_all | solution.py:34
  79.5 51.0 %all-to-all-done.1 = bf16[64,2,16,512]{3,2,1,0:T(8,128)(2,1)S(1)} async-done(((bf16[64,2,16,512]{3,2,1,0:T(8,128)(2,1)}), bf16[64,2,16,512]{3,2,1,0:T(8,128)(2,1)S(1)}, u32[]{:S(2)}, u32[]{:S(2)}) %all-to-all-start.1) | async-done | bytes 2097184 | tf_op jit(solution)/shard_map/all_to_all | solution.py:34
  130.6 1.4 copy.20
  132.0 1.7 fusion.4
  133.7 1.6 reshape.78
  135.6 10.5 %psum.21 = f32[896]{0:T(1024)S(1)} all-reduce(f32[896]{0:T(1024)S(1)} %multiply_reduce_fusion.2), channel_id=1, replica_groups=mesh['dp'=64,'mp'=8] {'mp'}, use_global_device_ids=true, to_apply=%region_2.0 | all-reduce | flops 896 | bytes 7168 | tf_op jit(solution)/shard_map/psum | solution.py:43
  146.1 39.0 %all-gather.5.cloned.1.call-done = bf16[512,2048]{0,1:T(8,128)(2,1)} async-done(((bf16[512,32]{0,1:T(8,128)(2,1)}), bf16[512,2048]{0,1:T(8,128)(2,1)}) %all-gather.5.cloned.1.call-update) | async-done | bytes 2097168 | tf_op jit(solution)/shard_map/all_gather | solution.py:46
  185.1 5.5 convolution_convert_fusion.2
  191.6 1.4 reshape.83
  193.1 138.0 %all-gather.9.cloned.1.call-done = bf16[7168,2048]{1,0:T(8,128)(2,1)} async-done(((bf16[896,2048]{1,0:T(8,128)(2,1)}), bf16[7168,2048]{1,0:T(8,128)(2,1)}) %all-gather.9.cloned.1.call-update) | async-done | bytes 29360144 | tf_op jit(solution)/shard_map/all_gather | solution.py:48
  331.0 12.7 %reduce_sum.68 = bf16[896,2048]{1,0:T(8,128)(2,1)} reduce(bf16[8,896,2048]{2,1,0:T(8,128)(2,1)} %bitcast.53, bf16[]{:T(256)} %constant.22.clone.1), dimensions={0}, to_apply=%region_3.0 | reduce | flops 12845056 | bytes 33030146 | tf_op jit(solution)/shard_map/reduce_sum | solution.py:48
  343.7 2.0 convert_add_fusion
  345.7 1.6 reshape.79
  347.4 1.0 multiply_reduce_fusion.4
  348.5 12.7 %multiply_reduce_fusion.3 = f32[896,2]{1,0:T(8,128)S(1)} fusion(f32[896,2,128]{2,1,0:T(2,128)S(1)} %copy-done.2, f32[896,2,128]{2,1,0:T(2,128)S(1)} %reshape.79, f32[896,2]{1,0:T(8,128)S(1)} %add_rsqrt_fusion), kind=kLoop, calls=%fused_computation.15 | loop fusion | flops 686336 | bytes 1849344 | tf_op jit(solution)/shard_map/reduce_sum | solution.py:57
  361.2 1.1 mul.123
  362.4 1.1 mul.118
  363.5 2.1 fusion.2
  365.6 39.9 %all-gather.7.cloned.1.call-done = bf16[896,2048]{1,0:T(8,128)(2,1)} async-done(((bf16[896,256]{1,0:T(8,128)(2,1)}), bf16[896,2048]{1,0:T(8,128)(2,1)}) %all-gather.7.cloned.1.call-update) | async-done | bytes 3670032 | tf_op jit(solution)/shard_map/all_gather | solution.py:59
  405.6 6.4 fusion.9
  412.0 6.2 multiply_reduce_fusion
  418.2 11.9 %psum.22 = f32[896]{0:T(1024)S(1)} all-reduce(f32[896]{0:T(1024)S(1)} %get-tuple-element.4), channel_id=1, replica_groups=mesh['dp'=64,'mp'=8] {'mp'}, use_global_device_ids=true, to_apply=%region_7.0 | all-reduce | flops 896 | bytes 7168 | tf_op jit(solution)/shard_map/psum | solution.py:72
  430.2 1.9 subtract_convert_fusion
  433.3 2.2 copy.23
  435.4 13.3 %all-to-all-start.2 = ((bf16[64,2,16,512]{3,2,1,0:T(8,128)(2,1)}), bf16[64,2,16,512]{3,2,1,0:T(8,128)(2,1)S(1)}, u32[]{:S(2)}, u32[]{:S(2)}) async-start(bf16[64,2,16,512]{3,2,1,0:T(8,128)(2,1)} %bitcast.26), calls=%async_computation.2 | async-start | bytes 4194304 | tf_op jit(solution)/shard_map/all_to_all | solution.py:79
  448.7 181.7 %psum.23 = f32[512]{0:T(512)} all-reduce(f32[512]{0:T(512)S(1)} %get-tuple-element.3), channel_id=1, replica_groups=mesh['dp'=64,'mp'=8] {'dp'}, use_global_device_ids=true, to_apply=%region_9.0 | all-reduce | flops 512 | bytes 4096 | tf_op jit(solution)/shard_map/psum | solution.py:76
  630.4 3.4 convolution_bitcast_fusion
  633.8 69.7 %reduce-scatter.2.cloned.1.call-done = f32[32,512]{1,0:T(8,128)} async-done(((f32[2048,512]{1,0:T(8,128)}), f32[32,512]{1,0:T(8,128)}) %reduce-scatter.2.cloned.1.call-update) | async-done | bytes 65552 | tf_op jit(solution)/shard_map/reduce_scatter | solution.py:60
  (35 shorter events, 4.9 us)
Async XLA Ops:
  7.2 61.4 %copy-start = (bf16[1,384,512]{2,1,0:T(8,128)(2,1)S(1)}, bf16[1,384,512]{2,1,0:T(8,128)(2,1)}, u32[]{:S(2)}) copy-start(bf16[1,384,512]{2,1,0:T(8,128)(2,1)} %param.9) | copy-start | bytes 1179652
  68.5 2.6 copy-start.5
  71.2 59.4 %all-to-all-start.1 = ((bf16[64,2,16,512]{3,2,1,0:T(8,128)(2,1)}), bf16[64,2,16,512]{3,2,1,0:T(8,128)(2,1)S(1)}, u32[]{:S(2)}, u32[]{:S(2)}) async-start(bf16[64,2,16,512]{3,2,1,0:T(8,128)(2,1)} %bitcast.62), calls=%async_computation.1 | async-start | bytes 4194304 | tf_op jit(solution)/shard_map/all_to_all | solution.py:34
  78.8 106.3 %all-gather.5.cloned.1.call-start = ((), (), s32[]{:S(2)}) async-start(), calls=%async_computation.4 | async-start | bytes 2129920 | tf_op jit(solution)/shard_map/all_gather | solution.py:46
  79.5 251.5 %all-gather.9.cloned.1.call-start = ((), (), s32[]{:S(2)}) async-start(), calls=%async_computation.7 | async-start | bytes 33030144 | tf_op jit(solution)/shard_map/all_gather | solution.py:48
  135.3 49.8 %copy-start.7 = (f32[512]{0:T(512)S(1)}, f32[512]{0:T(512)}, u32[]{:S(2)}) copy-start(f32[512]{0:T(512)} %param.10) | copy-start | bytes 6148
  190.6 1.0 copy-start.3
  190.7 214.9 %all-gather.7.cloned.1.call-start = ((), (), s32[]{:S(2)}) async-start(), calls=%async_computation.5 | async-start | bytes 4128768 | tf_op jit(solution)/shard_map/all_gather | solution.py:59
  331.0 12.7 %copy-start.6 = (f32[256]{0:T(256)S(1)}, f32[256]{0:T(256)}, u32[]{:S(2)}) copy-start(f32[256]{0:T(256)} %param.12) | copy-start | bytes 3076
  347.4 1.2 copy-start.2
  361.2 2.3 copy-start.4
  365.6 337.9 %reduce-scatter.2.cloned.1.call-start = ((), (), s32[]{:S(2)}) async-start(), calls=%async_computation.6 | async-start | bytes 4259840 | tf_op jit(solution)/shard_map/reduce_scatter | solution.py:60
  435.4 195.0 %all-to-all-start.2 = ((bf16[64,2,16,512]{3,2,1,0:T(8,128)(2,1)}), bf16[64,2,16,512]{3,2,1,0:T(8,128)(2,1)S(1)}, u32[]{:S(2)}, u32[]{:S(2)}) async-start(bf16[64,2,16,512]{3,2,1,0:T(8,128)(2,1)} %bitcast.26), calls=%async_computation.2 | async-start | bytes 4194304 | tf_op jit(solution)/shard_map/all_to_all | solution.py:79
  630.4 73.0 %copy-start.1 = (bf16[1,384,512]{2,1,0:T(8,128)(2,1)S(1)}, bf16[1,384,512]{2,1,0:T(8,128)(2,1)}, u32[]{:S(2)}) copy-start(bf16[1,384,512]{2,1,0:T(8,128)(2,1)} %param.9) | copy-start | bytes 1179652
Sparse Core Ops, SparseCore 0:
  82.7 102.3 all-gather.4
  190.8 140.1 all-gather.8
  365.7 39.8 all-gather.6
  412.1 291.3 reduce-scatter.1
